TPU v7x, 32 devices: a whole 2x2x4 slice. The times are simulated.
32 devices in a mesh: gx: 4 (over z), gy: 2 (over y), gz: 4 (over x, core).
Axes of the slice: x: 2, y: 2, z: 4, core: 2. Of those that a mesh axis runs over, the one named last changes fastest.
Arguments:
- points: float32 [1024, 3, 128], P(('gx', 'gy', 'gz'))
- charges: float32 [1024, 128], P(('gx', 'gy', 'gz')), may hold values from -0.6 to 0.6
- interpolant: float32 [1024, 64, 64], P(('gx', 'gy', 'gz')), may hold values from -0.75 to 0.75
- leaf_transfer: float32 [1024, 64, 64], P(('gx', 'gy', 'gz'))
- node_transfer: float32 [32, 5, 64, 64], P(('gx', 'gy', 'gz')), as said below
- node_points: float32 [32, 5, 3, 64], P(('gx', 'gy', 'gz')), as said below
- near_list: int32 [1024, 8], P(('gx', 'gy', 'gz')), may hold values from 0 to 47, as said below
- near_count: int32 [1024], P(('gx', 'gy', 'gz')), may hold values from 1 to 8, as said below
- far_list: int32 [1024, 8], P(('gx', 'gy', 'gz')), may hold values from 0 to 47, as said below
Outputs:
- potential: float32 [1024, 128], P(('gx', 'gy', 'gz'))
Inputs may be any that keep to these rules, and one draw needn't show every extreme that they name: `near_list`: entry 0 of the list of a leaf with number i within its device is i + 8; the other entries are distinct positions within 8 of i + 8. `far_list`: distinct positions within 8 of the leaf's own position i + 8, none of them in the leaf's near list. Only the first near_count[g] entries of leaf g's near list are used. `node_transfer`: rows of devices in the same node (k, c) are equal at level k. `node_points`: rows of devices in the same node (k, c) are equal at level k.
All inputs are finite; a program needn't handle non-finite values.
Results may differ from a plain program's by a relative error of at most 0.0003.
Values sent between devices are 32-bit elements; how exact they have to be, the bound alone decides.
A program may use at most 64 MiB of HBM per device.

v0:
```python
import jax
import jax.numpy as jnp
from jax import lax
from jax.sharding import PartitionSpec as P

HALO = 8


SOFTENING = 0.0625
HIGHEST = lax.Precision.HIGHEST


def padded(cells, sides, width):
    for axis, dim in sides:
        count = lax.axis_size(axis)
        ends = count - 1
        head = lax.slice_in_dim(cells, 0, width, axis=dim)
        tail = lax.slice_in_dim(cells, cells.shape[dim] - width, cells.shape[dim], axis=dim)
        cells = jnp.concatenate(
            [
                lax.ppermute(tail, axis, [(i, (i + 1) % count) for i in range(ends)]),
                cells,
                lax.ppermute(head, axis, [((i + 1) % count, i) for i in range(ends)]),
            ],
            axis=dim,
        )
    return cells


def partner(value, axis, distance):
    mask = 2**distance
    pairs = [(source, source ^ mask) for source in range(lax.axis_size(axis))]
    return lax.ppermute(value, axis, pairs)


def kernel(targets, sources):
    spread = targets[..., :, :, None] - sources[..., :, None, :]
    return lax.rsqrt(jnp.sum(spread * spread, axis=-3) + SOFTENING)


def leaf_terms(window, near_list, near_count, far_list, skeleton_rank):
    leaves = near_list.shape[0]
    margin = (window.shape[0] - leaves) // 2
    targets = window[margin : margin + leaves]
    blocks = leaves // 4

    def block_terms(pieces):
        target_block, near_block, count_block, far_block = pieces
        sources = window[near_block]
        slot_index = jnp.arange(near_block.shape[1], dtype=jnp.int32)
        is_live = slot_index[None, :] < count_block[:, None]
        weights = jnp.where(is_live[:, :, None], sources[:, :, 3, :], 0.0)
        kernel_tiles = kernel(target_block[:, None, 0:3, :], sources[:, :, 0:3, :])
        near_part = jnp.einsum("bmpq,bmq->bp", kernel_tiles, weights, precision=HIGHEST)
        distant = window[far_block]
        coupling = kernel(
            target_block[:, None, 0:3, :skeleton_rank], distant[:, :, 0:3, :skeleton_rank]
        )
        far_part = jnp.einsum(
            "bmpq,bmq->bp", coupling, distant[:, :, 4, :skeleton_rank], precision=HIGHEST
        )
        return (near_part, far_part)

    near_part, far_part = lax.map(
        block_terms,
        (
            targets.reshape((blocks, 4) + targets.shape[1:]),
            near_list.reshape(blocks, 4, near_list.shape[1]),
            near_count.reshape(blocks, 4),
            far_list.reshape(blocks, 4, far_list.shape[1]),
        ),
    )
    return (
        near_part.reshape(leaves, near_part.shape[2]),
        far_part.reshape(leaves, far_part.shape[2]),
    )


def on_device(
    points,
    charges,
    interpolant,
    leaf_transfer,
    node_transfer,
    node_points,
    near_list,
    near_count,
    far_list,
):
    skeleton_rank = interpolant.shape[1]
    leaf_points = points.shape[2]
    skeleton = charges[:, :skeleton_rank] + jnp.einsum(
        "lrp,lp->lr", interpolant, charges[:, skeleton_rank:], precision=HIGHEST
    )
    packed = jnp.concatenate(
        [
            points,
            charges[:, None, :],
            jnp.pad(skeleton, ((0, 0), (0, leaf_points - skeleton_rank)))[:, None, :],
        ],
        axis=1,
    )
    window = padded(packed, ((("gx", "gy", "gz"), 0),), HALO)
    device_skeleton = jnp.einsum("irc,ir->c", leaf_transfer, skeleton, precision=HIGHEST)
    transfers = node_transfer[0]
    centres = node_points[0]
    level_count = transfers.shape[0]
    couplings = []
    swappers = (
        (lax.axis_size("gz"), lambda payload, bit_place: partner(payload, "gz", bit_place)),
        (lax.axis_size("gy"), lambda payload, bit_place: partner(payload, "gy", bit_place)),
        (lax.axis_size("gx"), lambda payload, bit_place: partner(payload, "gx", bit_place)),
    )
    current = device_skeleton
    level_index = 0
    for axis_length, swapper in swappers:
        for bit_place in range(axis_length.bit_length() - 1):
            lifted = jnp.einsum("rc,r->c", transfers[level_index], current, precision=HIGHEST)
            payload = jnp.concatenate([current[None], lifted[None], centres[level_index]], axis=0)
            partner_data = swapper(payload, bit_place)
            couplings.append(
                jnp.dot(
                    kernel(centres[level_index], partner_data[2:5]),
                    partner_data[0],
                    precision=HIGHEST,
                )
            )
            current = lifted + partner_data[1]
            level_index = level_index + 1
    expansion = couplings[-1]
    for level_index in range(level_count - 1, 0, -1):
        expansion = couplings[level_index - 1] + jnp.dot(
            transfers[level_index - 1], expansion, precision=HIGHEST
        )
    from_device = jnp.einsum("irc,c->ir", leaf_transfer, expansion, precision=HIGHEST)
    near_part, far_part = leaf_terms(window, near_list, near_count, far_list, skeleton_rank)
    combined = far_part + from_device
    upper = jnp.einsum("lrp,lr->lp", interpolant, combined, precision=HIGHEST)
    return jnp.concatenate([combined, upper], axis=1) + near_part


def solution(mesh):
    return jax.shard_map(
        on_device,
        mesh=mesh,
        in_specs=(
            P(("gx", "gy", "gz"), None, None),
            P(("gx", "gy", "gz"), None),
            P(("gx", "gy", "gz"), None, None),
            P(("gx", "gy", "gz"), None, None),
            P(("gx", "gy", "gz"), None, None, None),
            P(("gx", "gy", "gz"), None, None, None),
            P(("gx", "gy", "gz"), None),
            P(("gx", "gy", "gz")),
            P(("gx", "gy", "gz"), None),
        ),
        out_specs=P(("gx", "gy", "gz"), None),
        check_vma=False,
    )
```

profile of v0, /device:TPU:0, one launch (start us, length us, event | category | flops | bytes accessed | tf_op | source)
XLA Modules:
  0.0 86.7 jit_solution(8170418632625923189)
XLA Ops:
  0.1 0.9 fusion.81
  0.9 0.8 slice.122
  1.7 1.7 %fusion.82 = f32[32,1,64]{2,1,0:T(1,128)S(1)} fusion(f32[32,64,64]{2,1,0:T(8,128)S(1)} %copy-done, f32[32,64,1]{1,2,0:T(1,128)S(1)} %bitcast.299), kind=kOutput, calls=%fused_computation.132 | convolution fusion | flops 1572864 | bytes 540672 | tf_op jit(solution)/shard_map/lrp,lp->lr/dot_general | solution.py:92
  3.4 0.7 slice_add_fusion
  4.2 1.9 %fusion.83 = f32[1,64,1]{1,0,2:T(1,128)S(1)} fusion(f32[32,64,1]{1,2,0:T(1,128)S(1)} %bitcast.295, f32[32,64,64]{2,1,0:T(8,128)} %param.14), kind=kOutput, calls=%fused_computation.133 | convolution fusion | flops 1572864 | bytes 532736 | tf_op jit(solution)/shard_map/irc,ir->c/dot_general | solution.py:104
  6.2 0.5 collective-permute-start.2
  6.8 2.0 %collective-permute-start = (f32[8,5,128]{2,1,0:T(8,128)S(1)}, f32[8,5,128]{2,1,0:T(8,128)S(1)}, u32[]{:S(2)}, u32[]{:S(2)}) collective-permute-start(f32[8,5,128]{2,1,0:T(8,128)S(1)} %get-tuple-element.68), channel_id=1, source_target_pairs={{0,1},{1,2},{2,3},{3,4},{4,5},{5,6},{6,7},{7,8},{8,9},{9,10},{10,1... | collective-permute-start | bytes 61448 | tf_op jit(solution)/shard_map/ppermute | solution.py:21
  8.8 1.3 %collective-permute-start.1 = (f32[8,5,128]{2,1,0:T(8,128)S(1)}, f32[8,5,128]{2,1,0:T(8,128)S(1)}, u32[]{:S(2)}, u32[]{:S(2)}) collective-permute-start(f32[8,5,128]{2,1,0:T(8,128)S(1)} %get-tuple-element.69), channel_id=1, source_target_pairs={{1,0},{2,1},{3,2},{4,3},{5,4},{6,5},{7,6},{8,7},{9,8},{10,9},{11,1... | collective-permute-start | bytes 61448 | tf_op jit(solution)/shard_map/ppermute | solution.py:23
  10.6 4.9 %collective-permute-start.3 = (f32[5,64]{1,0:T(8,128)S(1)}, f32[5,64]{1,0:T(8,128)S(1)}, u32[]{:S(2)}, u32[]{:S(2)}) collective-permute-start(f32[5,64]{1,0:T(8,128)S(1)} %pad_maximum_fusion.6), channel_id=1, source_target_pairs={{0,2},{1,3},{2,0},{3,1},{4,6},{5,7},{6,4},{7,5},{8,10},{9,11},{10,... | collective-permute-start | bytes 3848 | tf_op jit(solution)/shard_map/ppermute | solution.py:33
  15.6 1.5 %collective-permute-done.3 = f32[5,64]{1,0:T(8,128)S(1)} collective-permute-done((f32[5,64]{1,0:T(8,128)S(1)}, f32[5,64]{1,0:T(8,128)S(1)}, u32[]{:S(2)}, u32[]{:S(2)}) %collective-permute-start.3) | collective-permute-done | bytes 1312 | tf_op jit(solution)/shard_map/ppermute | solution.py:33
  17.2 3.0 %collective-permute-start.4 = (f32[5,64]{1,0:T(8,128)S(1)}, f32[5,64]{1,0:T(8,128)S(1)}, u32[]{:S(2)}, u32[]{:S(2)}) collective-permute-start(f32[5,64]{1,0:T(8,128)S(1)} %pad_maximum_fusion.7), channel_id=1, source_target_pairs={{0,4},{4,0},{1,5},{5,1},{2,6},{6,2},{3,7},{7,3},{8,12},{12,8},{9,1... | collective-permute-start | bytes 3848 | tf_op jit(solution)/shard_map/ppermute | solution.py:33
  20.4 1.5 %collective-permute-done.4 = f32[5,64]{1,0:T(8,128)S(1)} collective-permute-done((f32[5,64]{1,0:T(8,128)S(1)}, f32[5,64]{1,0:T(8,128)S(1)}, u32[]{:S(2)}, u32[]{:S(2)}) %collective-permute-start.4) | collective-permute-done | bytes 1312 | tf_op jit(solution)/shard_map/ppermute | solution.py:33
  22.0 3.0 %collective-permute-start.5 = (f32[5,64]{1,0:T(8,128)S(1)}, f32[5,64]{1,0:T(8,128)S(1)}, u32[]{:S(2)}, u32[]{:S(2)}) collective-permute-start(f32[5,64]{1,0:T(8,128)S(1)} %pad_maximum_fusion.8), channel_id=1, source_target_pairs={{0,8},{8,0},{16,24},{24,16},{1,9},{9,1},{17,25},{25,17},{2,10},{10... | collective-permute-start | bytes 3848 | tf_op jit(solution)/shard_map/ppermute | solution.py:33
  25.1 1.5 %collective-permute-done.5 = f32[5,64]{1,0:T(8,128)S(1)} collective-permute-done((f32[5,64]{1,0:T(8,128)S(1)}, f32[5,64]{1,0:T(8,128)S(1)}, u32[]{:S(2)}, u32[]{:S(2)}) %collective-permute-start.5) | collective-permute-done | bytes 1312 | tf_op jit(solution)/shard_map/ppermute | solution.py:33
  26.8 3.1 %collective-permute-start.6 = (f32[5,64]{1,0:T(8,128)S(1)}, f32[5,64]{1,0:T(8,128)S(1)}, u32[]{:S(2)}, u32[]{:S(2)}) collective-permute-start(f32[5,64]{1,0:T(8,128)S(1)} %pad_maximum_fusion.9), channel_id=1, source_target_pairs={{0,16},{8,24},{16,0},{24,8},{1,17},{9,25},{17,1},{25,9},{2,18},{10... | collective-permute-start | bytes 3848 | tf_op jit(solution)/shard_map/ppermute | solution.py:33
  30.0 1.5 %collective-permute-done.6 = f32[5,64]{1,0:T(8,128)S(1)} collective-permute-done((f32[5,64]{1,0:T(8,128)S(1)}, f32[5,64]{1,0:T(8,128)S(1)}, u32[]{:S(2)}, u32[]{:S(2)}) %collective-permute-start.6) | collective-permute-done | bytes 1312 | tf_op jit(solution)/shard_map/ppermute | solution.py:33
  33.2 2.5 %fusion.84 = f32[1,32,64]{2,0,1:T(1,128)S(1)} fusion(f32[64,1,1]{0,1,2:T(1,128)S(1)} %fusion.18, f32[32,64,64]{2,1,0:T(8,128)S(1)} %copy-done.1), kind=kOutput, calls=%fused_computation.134 | convolution fusion | flops 1572864 | bytes 532736 | tf_op jit(solution)/shard_map/irc,c->ir/dot_general | solution.py:135
  35.8 49.2 %while.12 = (s32[]{:T(128)}, f32[8,4,128]{2,1,0:T(4,128)S(1)}, f32[8,4,64]{2,1,0:T(4,128)S(1)}, f32[8,4,5,128]{3,2,1,0:T(8,128)S(1)}, s32[8,4,8]{2,1,0:T(4,128)S...) while((s32[]{:T(128)}, f32[8,4,128]{2,1,0:T(4,128)S(1)}, ...), condition=%wide.region_3.4_spmd, body=%wide.region_0.3_spmd.sunk | while | flops 13768930 | bytes 6483689 | solution.py:64
  36.1 0.6 gather_fusion
  36.9 0.6 gather_fusion.1
  37.5 0.5 multiply_reduce_fusion.10
  38.0 1.1 %fusion.110 = f32[4,1,64,1]{2,1,3,0:T(1,128)S(1)} fusion(f32[4,8,64,64]{3,2,1,0:T(8,128)S(1)} %multiply_reduce_fusion.10, f32[4,8,5,128]{3,2,1,0:T(8,128)S(1)} %bitcast.281), kind=kOutput, calls=%fused_computation.7.clone.1 | convolution fusion | flops 1703936 | bytes 1065984 | tf_op jit(solution)/shard_map/while/body/eval_jaxpr/bmpq,bmq->bp/dot_general | solution.py:59
  39.1 0.8 multiply_reduce_fusion.9
  39.9 2.0 %fusion.109 = f32[4,1,128,1]{2,1,3,0:T(1,128)S(1)} fusion(f32[4,8,128,1]{2,3,1,0:T(1,128)S(1)} %bitcast.284, f32[4,8,128,128]{3,2,1,0:T(8,128)S(1)} %multiply_reduce_fusion.9), kind=kOutput, calls=%fused_computation.4.clone.1 | convolution fusion | flops 6815744 | bytes 2115584 | tf_op jit(solution)/shard_map/while/body/eval_jaxpr/bmpq,bmq->bp/dot_general | solution.py:54
  42.3 0.6 gather_fusion
  43.0 0.6 gather_fusion.1
  43.6 0.5 multiply_reduce_fusion.10
  44.1 1.1 %fusion.110 = f32[4,1,64,1]{2,1,3,0:T(1,128)S(1)} fusion(f32[4,8,64,64]{3,2,1,0:T(8,128)S(1)} %multiply_reduce_fusion.10, f32[4,8,5,128]{3,2,1,0:T(8,128)S(1)} %bitcast.281), kind=kOutput, calls=%fused_computation.7.clone.1 | convolution fusion | flops 1703936 | bytes 1065984 | tf_op jit(solution)/shard_map/while/body/eval_jaxpr/bmpq,bmq->bp/dot_general | solution.py:59
  45.3 0.8 multiply_reduce_fusion.9
  46.0 2.0 %fusion.109 = f32[4,1,128,1]{2,1,3,0:T(1,128)S(1)} fusion(f32[4,8,128,1]{2,3,1,0:T(1,128)S(1)} %bitcast.284, f32[4,8,128,128]{3,2,1,0:T(8,128)S(1)} %multiply_reduce_fusion.9), kind=kOutput, calls=%fused_computation.4.clone.1 | convolution fusion | flops 6815744 | bytes 2115584 | tf_op jit(solution)/shard_map/while/body/eval_jaxpr/bmpq,bmq->bp/dot_general | solution.py:54
  48.4 0.6 gather_fusion
  49.2 0.6 gather_fusion.1
  49.8 0.5 multiply_reduce_fusion.10
  50.3 1.1 %fusion.110 = f32[4,1,64,1]{2,1,3,0:T(1,128)S(1)} fusion(f32[4,8,64,64]{3,2,1,0:T(8,128)S(1)} %multiply_reduce_fusion.10, f32[4,8,5,128]{3,2,1,0:T(8,128)S(1)} %bitcast.281), kind=kOutput, calls=%fused_computation.7.clone.1 | convolution fusion | flops 1703936 | bytes 1065984 | tf_op jit(solution)/shard_map/while/body/eval_jaxpr/bmpq,bmq->bp/dot_general | solution.py:59
  51.4 0.8 multiply_reduce_fusion.9
  52.2 2.0 %fusion.109 = f32[4,1,128,1]{2,1,3,0:T(1,128)S(1)} fusion(f32[4,8,128,1]{2,3,1,0:T(1,128)S(1)} %bitcast.284, f32[4,8,128,128]{3,2,1,0:T(8,128)S(1)} %multiply_reduce_fusion.9), kind=kOutput, calls=%fused_computation.4.clone.1 | convolution fusion | flops 6815744 | bytes 2115584 | tf_op jit(solution)/shard_map/while/body/eval_jaxpr/bmpq,bmq->bp/dot_general | solution.py:54
  54.6 0.6 gather_fusion
  55.3 0.6 gather_fusion.1
  55.9 0.5 multiply_reduce_fusion.10
  56.4 1.1 %fusion.110 = f32[4,1,64,1]{2,1,3,0:T(1,128)S(1)} fusion(f32[4,8,64,64]{3,2,1,0:T(8,128)S(1)} %multiply_reduce_fusion.10, f32[4,8,5,128]{3,2,1,0:T(8,128)S(1)} %bitcast.281), kind=kOutput, calls=%fused_computation.7.clone.1 | convolution fusion | flops 1703936 | bytes 1065984 | tf_op jit(solution)/shard_map/while/body/eval_jaxpr/bmpq,bmq->bp/dot_general | solution.py:59
  57.6 0.8 multiply_reduce_fusion.9
  58.3 2.0 %fusion.109 = f32[4,1,128,1]{2,1,3,0:T(1,128)S(1)} fusion(f32[4,8,128,1]{2,3,1,0:T(1,128)S(1)} %bitcast.284, f32[4,8,128,128]{3,2,1,0:T(8,128)S(1)} %multiply_reduce_fusion.9), kind=kOutput, calls=%fused_computation.4.clone.1 | convolution fusion | flops 6815744 | bytes 2115584 | tf_op jit(solution)/shard_map/while/body/eval_jaxpr/bmpq,bmq->bp/dot_general | solution.py:54
  60.7 0.6 gather_fusion
  61.5 0.6 gather_fusion.1
  62.6 1.1 %fusion.110 = f32[4,1,64,1]{2,1,3,0:T(1,128)S(1)} fusion(f32[4,8,64,64]{3,2,1,0:T(8,128)S(1)} %multiply_reduce_fusion.10, f32[4,8,5,128]{3,2,1,0:T(8,128)S(1)} %bitcast.281), kind=kOutput, calls=%fused_computation.7.clone.1 | convolution fusion | flops 1703936 | bytes 1065984 | tf_op jit(solution)/shard_map/while/body/eval_jaxpr/bmpq,bmq->bp/dot_general | solution.py:59
  63.7 0.8 multiply_reduce_fusion.9
  64.5 2.0 %fusion.109 = f32[4,1,128,1]{2,1,3,0:T(1,128)S(1)} fusion(f32[4,8,128,1]{2,3,1,0:T(1,128)S(1)} %bitcast.284, f32[4,8,128,128]{3,2,1,0:T(8,128)S(1)} %multiply_reduce_fusion.9), kind=kOutput, calls=%fused_computation.4.clone.1 | convolution fusion | flops 6815744 | bytes 2115584 | tf_op jit(solution)/shard_map/while/body/eval_jaxpr/bmpq,bmq->bp/dot_general | solution.py:54
  66.9 0.6 gather_fusion
  67.6 0.6 gather_fusion.1
  68.7 1.1 %fusion.110 = f32[4,1,64,1]{2,1,3,0:T(1,128)S(1)} fusion(f32[4,8,64,64]{3,2,1,0:T(8,128)S(1)} %multiply_reduce_fusion.10, f32[4,8,5,128]{3,2,1,0:T(8,128)S(1)} %bitcast.281), kind=kOutput, calls=%fused_computation.7.clone.1 | convolution fusion | flops 1703936 | bytes 1065984 | tf_op jit(solution)/shard_map/while/body/eval_jaxpr/bmpq,bmq->bp/dot_general | solution.py:59
  69.9 0.8 multiply_reduce_fusion.9
  70.7 2.0 %fusion.109 = f32[4,1,128,1]{2,1,3,0:T(1,128)S(1)} fusion(f32[4,8,128,1]{2,3,1,0:T(1,128)S(1)} %bitcast.284, f32[4,8,128,128]{3,2,1,0:T(8,128)S(1)} %multiply_reduce_fusion.9), kind=kOutput, calls=%fused_computation.4.clone.1 | convolution fusion | flops 6815744 | bytes 2115584 | tf_op jit(solution)/shard_map/while/body/eval_jaxpr/bmpq,bmq->bp/dot_general | solution.py:54
  73.0 0.6 gather_fusion
  73.8 0.6 gather_fusion.1
  74.9 1.1 %fusion.110 = f32[4,1,64,1]{2,1,3,0:T(1,128)S(1)} fusion(f32[4,8,64,64]{3,2,1,0:T(8,128)S(1)} %multiply_reduce_fusion.10, f32[4,8,5,128]{3,2,1,0:T(8,128)S(1)} %bitcast.281), kind=kOutput, calls=%fused_computation.7.clone.1 | convolution fusion | flops 1703936 | bytes 1065984 | tf_op jit(solution)/shard_map/while/body/eval_jaxpr/bmpq,bmq->bp/dot_general | solution.py:59
  76.0 0.8 multiply_reduce_fusion.9
  76.8 2.0 %fusion.109 = f32[4,1,128,1]{2,1,3,0:T(1,128)S(1)} fusion(f32[4,8,128,1]{2,3,1,0:T(1,128)S(1)} %bitcast.284, f32[4,8,128,128]{3,2,1,0:T(8,128)S(1)} %multiply_reduce_fusion.9), kind=kOutput, calls=%fused_computation.4.clone.1 | convolution fusion | flops 6815744 | bytes 2115584 | tf_op jit(solution)/shard_map/while/body/eval_jaxpr/bmpq,bmq->bp/dot_general | solution.py:54
  79.2 0.6 gather_fusion
  79.9 0.6 gather_fusion.1
  81.0 1.1 %fusion.110 = f32[4,1,64,1]{2,1,3,0:T(1,128)S(1)} fusion(f32[4,8,64,64]{3,2,1,0:T(8,128)S(1)} %multiply_reduce_fusion.10, f32[4,8,5,128]{3,2,1,0:T(8,128)S(1)} %bitcast.281), kind=kOutput, calls=%fused_computation.7.clone.1 | convolution fusion | flops 1703936 | bytes 1065984 | tf_op jit(solution)/shard_map/while/body/eval_jaxpr/bmpq,bmq->bp/dot_general | solution.py:59
  82.2 0.8 multiply_reduce_fusion.9
  83.0 2.0 %fusion.109 = f32[4,1,128,1]{2,1,3,0:T(1,128)S(1)} fusion(f32[4,8,128,1]{2,3,1,0:T(1,128)S(1)} %bitcast.284, f32[4,8,128,128]{3,2,1,0:T(8,128)S(1)} %multiply_reduce_fusion.9), kind=kOutput, calls=%fused_computation.4.clone.1 | convolution fusion | flops 6815744 | bytes 2115584 | tf_op jit(solution)/shard_map/while/body/eval_jaxpr/bmpq,bmq->bp/dot_general | solution.py:54
  85.0 1.0 %fusion.85 = f32[32,1,64]{2,1,0:T(1,128)S(1)} fusion(f32[32,64,1]{1,2,0:T(1,128)S(1)} %bitcast.296, f32[32,64,64]{2,1,0:T(8,128)S(1)} %copy-done), kind=kOutput, calls=%fused_computation.135 | convolution fusion | flops 1572864 | bytes 540672 | tf_op jit(solution)/shard_map/lrp,lr->lp/dot_general | solution.py:138
  86.0 0.7 maximum_add_fusion
  (200 shorter events, 8.8 us)
Async XLA Ops:
  0.0 1.7 %copy-start = (f32[32,64,64]{2,1,0:T(8,128)S(1)}, f32[32,64,64]{2,1,0:T(8,128)}, u32[]{:S(2)}) copy-start(f32[32,64,64]{2,1,0:T(8,128)} %param.13) | copy-start | bytes 1572868
  0.0 6.8 %copy-start.3 = (f32[32,128]{1,0:T(8,128)S(1)}, f32[32,128]{1,0:T(8,128)}, u32[]{:S(2)}) copy-start(f32[32,128]{1,0:T(8,128)} %param.12) | copy-start | bytes 49156
  0.0 33.2 %copy-start.1 = (f32[32,64,64]{2,1,0:T(8,128)S(1)}, f32[32,64,64]{2,1,0:T(8,128)}, u32[]{:S(2)}) copy-start(f32[32,64,64]{2,1,0:T(8,128)} %param.14) | copy-start | bytes 1572868
  0.0 6.0 %copy-start.2 = (f32[1,5,64,64]{3,2,1,0:T(8,128)S(1)}, f32[1,5,64,64]{3,2,1,0:T(8,128)}, u32[]{:S(2)}) copy-start(f32[1,5,64,64]{3,2,1,0:T(8,128)} %param.15) | copy-start | bytes 245764
  0.0 6.7 %copy-start.4 = (f32[32,3,128]{2,0,1:T(8,128)S(1)}, f32[32,3,128]{2,0,1:T(8,128)}, u32[]{:S(2)}) copy-start(f32[32,3,128]{2,0,1:T(8,128)} %param.11) | copy-start | bytes 147460
  0.0 10.1 %copy-start.7 = (s32[32]{0:T(128)S(1)}, s32[32]{0:T(128)}, u32[]{:S(2)}) copy-start(s32[32]{0:T(128)} %param.18) | copy-start | bytes 388
  0.0 10.2 %copy-start.5 = (s32[32,8]{0,1:T(8,128)S(1)}, s32[32,8]{0,1:T(8,128)}, u32[]{:S(2)}) copy-start(s32[32,8]{0,1:T(8,128)} %param.17) | copy-start | bytes 3076
  0.0 10.3 %copy-start.6 = (s32[32,8]{0,1:T(8,128)S(1)}, s32[32,8]{0,1:T(8,128)}, u32[]{:S(2)}) copy-start(s32[32,8]{0,1:T(8,128)} %param.19) | copy-start | bytes 3076
  6.2 4.2 %collective-permute-start.2 = (f32[5,64]{1,0:T(8,128)S(1)}, f32[5,64]{1,0:T(8,128)S(1)}, u32[]{:S(2)}, u32[]{:S(2)}) collective-permute-start(f32[5,64]{1,0:T(8,128)S(1)} %pad_maximum_fusion.5), channel_id=1, source_target_pairs={{0,1},{1,0},{2,3},{3,2},{4,5},{5,4},{6,7},{7,6},{8,9},{9,8},{10,11... | collective-permute-start | bytes 3848 | tf_op jit(solution)/shard_map/ppermute | solution.py:33
  6.8 28.9 %collective-permute-start = (f32[8,5,128]{2,1,0:T(8,128)S(1)}, f32[8,5,128]{2,1,0:T(8,128)S(1)}, u32[]{:S(2)}, u32[]{:S(2)}) collective-permute-start(f32[8,5,128]{2,1,0:T(8,128)S(1)} %get-tuple-element.68), channel_id=1, source_target_pairs={{0,1},{1,2},{2,3},{3,4},{4,5},{5,6},{6,7},{7,8},{8,9},{9,10},{10,1... | collective-permute-start | bytes 61448 | tf_op jit(solution)/shard_map/ppermute | solution.py:21
  8.8 26.9 %collective-permute-start.1 = (f32[8,5,128]{2,1,0:T(8,128)S(1)}, f32[8,5,128]{2,1,0:T(8,128)S(1)}, u32[]{:S(2)}, u32[]{:S(2)}) collective-permute-start(f32[8,5,128]{2,1,0:T(8,128)S(1)} %get-tuple-element.69), channel_id=1, source_target_pairs={{1,0},{2,1},{3,2},{4,3},{5,4},{6,5},{7,6},{8,7},{9,8},{10,9},{11,1... | collective-permute-start | bytes 61448 | tf_op jit(solution)/shard_map/ppermute | solution.py:23
  10.6 6.5 %collective-permute-start.3 = (f32[5,64]{1,0:T(8,128)S(1)}, f32[5,64]{1,0:T(8,128)S(1)}, u32[]{:S(2)}, u32[]{:S(2)}) collective-permute-start(f32[5,64]{1,0:T(8,128)S(1)} %pad_maximum_fusion.6), channel_id=1, source_target_pairs={{0,2},{1,3},{2,0},{3,1},{4,6},{5,7},{6,4},{7,5},{8,10},{9,11},{10,... | collective-permute-start | bytes 3848 | tf_op jit(solution)/shard_map/ppermute | solution.py:33
  17.2 4.6 %collective-permute-start.4 = (f32[5,64]{1,0:T(8,128)S(1)}, f32[5,64]{1,0:T(8,128)S(1)}, u32[]{:S(2)}, u32[]{:S(2)}) collective-permute-start(f32[5,64]{1,0:T(8,128)S(1)} %pad_maximum_fusion.7), channel_id=1, source_target_pairs={{0,4},{4,0},{1,5},{5,1},{2,6},{6,2},{3,7},{7,3},{8,12},{12,8},{9,1... | collective-permute-start | bytes 3848 | tf_op jit(solution)/shard_map/ppermute | solution.py:33
  22.0 4.6 %collective-permute-start.5 = (f32[5,64]{1,0:T(8,128)S(1)}, f32[5,64]{1,0:T(8,128)S(1)}, u32[]{:S(2)}, u32[]{:S(2)}) collective-permute-start(f32[5,64]{1,0:T(8,128)S(1)} %pad_maximum_fusion.8), channel_id=1, source_target_pairs={{0,8},{8,0},{16,24},{24,16},{1,9},{9,1},{17,25},{25,17},{2,10},{10... | collective-permute-start | bytes 3848 | tf_op jit(solution)/shard_map/ppermute | solution.py:33
  26.8 4.7 %collective-permute-start.6 = (f32[5,64]{1,0:T(8,128)S(1)}, f32[5,64]{1,0:T(8,128)S(1)}, u32[]{:S(2)}, u32[]{:S(2)}) collective-permute-start(f32[5,64]{1,0:T(8,128)S(1)} %pad_maximum_fusion.9), channel_id=1, source_target_pairs={{0,16},{8,24},{16,0},{24,8},{1,17},{9,25},{17,1},{25,9},{2,18},{10... | collective-permute-start | bytes 3848 | tf_op jit(solution)/shard_map/ppermute | solution.py:33
where the time goes:
time: 87.1 us; the launch traced here: 86.7 us
  matrix products  34.6 us (40%)
  starting transfers between devices  17.8 us (20%)
  other arithmetic  13.8 us (16%)
  local copies, waits for them, and re-layouts  13.5 us (15%)
  waiting for transfers between devices  5.93 us (7%)
    dot_general x8, matrix products, block_terms(): jnp.einsum('bmpq,bmq->bp', kernel_tiles, weights, precision=HIGHEST)  16.3 us
    ppermute x5, starting transfers between devices, partner(): return lax.ppermute(value, axis, pairs)  14.6 us
    reduce_sum x21, other arithmetic, kernel(): return lax.rsqrt(jnp.sum(spread * spread, axis=-3) + SOFTENING)  10.7 us
    dot_general x8, matrix products, block_terms(): jnp.einsum('bmpq,bmq->bp', coupling, distant[:, :, 4, :skeleton_rank], pr...  8.91 us
    ppermute x5, waiting for transfers between devices, partner(): return lax.ppermute(value, axis, pairs)  5.93 us
    gather x8, local copies, waits for them, and re-layouts, block_terms(): sources = window[near_block]  4.68 us
    gather x8, local copies, waits for them, and re-layouts, block_terms(): distant = window[far_block]  4.68 us
    dot_general x1, matrix products, on_device(): jnp.einsum('irc,c->ir', leaf_transfer, expansion, precision=HIGHEST)  2.54 us
  transfers between devices with their start and end apart: 7, of which 4 were waited for; matrix products, arithmetic and copies ran while one was open for 6% of the time, Pallas kernels for 0%

commit v1 on v0

v1 whole, which is shorter than its diff:
```python
import functools
import math

import jax
import jax.numpy as jnp
from jax import lax
from jax.experimental import pallas as pl
from jax.experimental.pallas import tpu as pltpu
from jax.sharding import PartitionSpec as P

HALO = 8
SOFTENING = 0.0625
MESH = pl.DeviceIdType.MESH
AXES = ("gx", "gy", "gz")
CHUNK = 32


def flipped(place, mask):
    result = place
    bit = 1
    while bit <= mask:
        if mask & bit:
            result = result + bit - 2 * bit * ((place // bit) % 2)
        bit *= 2
    return result


def total_lanes(value):
    return jnp.sum(value, axis=1, keepdims=True)


def total_rows(value):
    return jnp.sum(value, axis=0, keepdims=True)


def softened(tx, ty, tz, sx, sy, sz):
    dx = tx - sx
    dy = ty - sy
    dz = tz - sz
    return lax.rsqrt(dx * dx + dy * dy + dz * dz + SOFTENING)


def body(
    sizes,
    near_ref,
    count_ref,
    far_ref,
    points_ref,
    charges_ref,
    interp_hbm,
    transfer_hbm,
    node_transfer_ref,
    node_points_ref,
    out_ref,
    interp_ref,
    transfer_ref,
    turned_ref,
    own_ref,
    win_ref,
    column_ref,
    far_acc_ref,
    coupling_ref,
    node_col_ref,
    pay_ref,
    recv_ref,
    load_sem,
    halo_send,
    halo_recv,
    tree_send,
    tree_recv,
):
    leaves, _, pts = points_ref.shape
    rank = interp_ref.shape[1]
    near_slots = near_ref.shape[1]
    far_slots = far_ref.shape[1]
    levels = node_transfer_ref.shape[1]
    gx, gy, gz = (lax.axis_index(name) for name in AXES)
    nx, ny, nz = sizes
    count = nx * ny * nz
    me = (gx * ny + gy) * nz + gz
    where_of = {"gx": gx, "gy": gy, "gz": gz}
    size_of = dict(zip(AXES, sizes))
    phases = [name for name in ("gz", "gy", "gx") if size_of[name] > 1]

    def address(index):
        return {
            "gx": index // (ny * nz),
            "gy": (index // nz) % ny,
            "gz": index % nz,
        }

    left = address((me + count - 1) % count)
    right = address((me + 1) % count)

    interp_copy = pltpu.make_async_copy(interp_hbm, interp_ref, load_sem.at[0])
    transfer_copy = pltpu.make_async_copy(transfer_hbm, transfer_ref, load_sem.at[1])
    interp_copy.start()
    transfer_copy.start()

    barrier = pltpu.get_barrier_semaphore()
    greeted = 2
    pl.semaphore_signal(barrier, inc=1, device_id=left, device_id_type=MESH)
    pl.semaphore_signal(barrier, inc=1, device_id=right, device_id_type=MESH)
    for name in phases:
        for mask in range(1, size_of[name]):
            pl.semaphore_signal(
                barrier,
                inc=1,
                device_id={name: flipped(where_of[name], mask)},
                device_id_type=MESH,
            )
            greeted += 1

    def unit(n):
        return (
            lax.broadcasted_iota(jnp.int32, (n, n), 0)
            == lax.broadcasted_iota(jnp.int32, (n, n), 1)
        ).astype(jnp.float32)

    eye = unit(rank)
    eye_pts = unit(pts)

    turned_ref[...] = jnp.concatenate(
        [charges_ref[:, rank:], charges_ref[:, :rank]], axis=1
    )
    own_ref[...] = jnp.zeros_like(own_ref)
    pay_ref[...] = jnp.zeros_like(pay_ref)
    own_ref[HALO : HALO + leaves, 0:3, :] = points_ref[...]

    for level in range(levels):
        for dim in range(3):
            node_col_ref[3 * level + dim] = jnp.broadcast_to(
                total_lanes(eye * node_points_ref[0, level, dim : dim + 1, :]), (rank, rank)
            )

    interp_copy.wait()
    transfer_copy.wait()

    def skeleton_step(step, acc):
        for part in range(4):
            leaf = step * 4 + part
            upper = turned_ref[pl.ds(leaf, 1), :]
            row = charges_ref[pl.ds(leaf, 1), :]
            col = total_lanes(interp_ref[leaf] * upper[:, :rank] + eye * row[:, :rank])
            own_ref[HALO + leaf, 3:4, :] = row
            own_ref[HALO + leaf, 4:5, 0:rank] = total_rows(eye * col)
            acc = acc + transfer_ref[leaf] * col
        return acc

    acc = lax.fori_loop(0, leaves // 4, skeleton_step, jnp.zeros((rank, rank), jnp.float32))
    node_row = total_rows(acc)

    pl.semaphore_wait(barrier, greeted)
    halo_copies = [
        pltpu.make_async_remote_copy(
            src_ref=own_ref.at[pl.ds(HALO, HALO)],
            dst_ref=win_ref.at[pl.ds(leaves + HALO, HALO)],
            send_sem=halo_send.at[0],
            recv_sem=halo_recv.at[0],
            device_id=left,
            device_id_type=MESH,
        ),
        pltpu.make_async_remote_copy(
            src_ref=own_ref.at[pl.ds(leaves, HALO)],
            dst_ref=win_ref.at[pl.ds(0, HALO)],
            send_sem=halo_send.at[1],
            recv_sem=halo_recv.at[1],
            device_id=right,
            device_id_type=MESH,
        ),
    ]
    for copy in halo_copies:
        copy.start()
    win_ref[HALO : HALO + leaves] = own_ref[HALO : HALO + leaves]

    def set_targets(leaf):
        tile = jnp.transpose(own_ref[HALO + leaf])
        for dim in range(3):
            column_ref[dim] = jnp.broadcast_to(tile[:, dim : dim + 1], (pts, pts))

    low_half = lax.broadcasted_iota(jnp.int32, (8, pts), 1) < rank

    def leaf_step(source_ref, leaf):
        set_targets(leaf)
        live = count_ref[leaf]
        places = [near_ref[leaf, m] for m in range(near_slots)]
        weights = [
            jnp.where(m < live, source_ref[places[m], 3:4, :], 0.0) for m in range(near_slots)
        ]
        near_cols = []
        for start in range(0, pts, CHUNK):
            tx, ty, tz = (column_ref[dim, start : start + CHUNK, :] for dim in range(3))
            total = jnp.zeros((CHUNK, pts), jnp.float32)
            for m in range(near_slots):
                sx, sy, sz = (source_ref[places[m], dim : dim + 1, :] for dim in range(3))
                total = total + softened(tx, ty, tz, sx, sy, sz) * weights[m]
            near_cols.append(total_lanes(total))
        near_col = jnp.concatenate(near_cols, axis=0)
        out_ref[pl.ds(leaf, 1), :] = total_rows(eye_pts * near_col)
        pairs = []
        for m in range(0, far_slots, 2):
            first = source_ref[far_ref[leaf, m]]
            second = source_ref[far_ref[leaf, m + 1]]
            pairs.append(jnp.where(low_half, first, pltpu.roll(second, rank, 1)))
        for start in range(0, rank, CHUNK):
            tx, ty, tz = (column_ref[dim, start : start + CHUNK, :] for dim in range(3))
            total = jnp.zeros((CHUNK, pts), jnp.float32)
            for pair in pairs:
                total = total + softened(
                    tx, ty, tz, pair[0:1], pair[1:2], pair[2:3]
                ) * pair[4:5]
            far_acc_ref[leaf, start : start + CHUNK, :] = total

    def run_leaves(source_ref, first, last):
        def step(leaf, carry):
            leaf_step(source_ref, leaf)
            return carry

        lax.fori_loop(first, last, step, 0)

    inner = leaves - 2 * HALO
    level = 0
    pay_at = 0
    recv_at = 0
    for order, name in enumerate(phases):
        bits = size_of[name].bit_length() - 1
        last_phase = order == len(phases) - 1
        chain = [node_row]
        for step in range(bits):
            if last_phase and step == bits - 1:
                chain.append(chain[-1])
            else:
                col = total_lanes(eye * chain[-1])
                chain.append(total_rows(node_transfer_ref[0, level + step] * col))
        for step in range(bits):
            pay_ref[pay_at + step, 0:1, 0:rank] = chain[step]
            pay_ref[pay_at + step, 1:4, 0:rank] = node_points_ref[0, level + step]
            pay_ref[pay_at + step, 4:5, 0:rank] = chain[bits]
        copies = []
        for mask in range(1, size_of[name]):
            step = mask.bit_length() - 1
            slot = recv_at + mask - 1
            copy = pltpu.make_async_remote_copy(
                src_ref=pay_ref.at[pay_at + step],
                dst_ref=recv_ref.at[slot],
                send_sem=tree_send.at[slot],
                recv_sem=tree_recv.at[slot],
                device_id={name: flipped(where_of[name], mask)},
                device_id_type=MESH,
            )
            copy.start()
            copies.append(copy)
        first = HALO + inner * order // len(phases)
        last = HALO + inner * (order + 1) // len(phases)
        run_leaves(own_ref, first, last)
        if last_phase:
            for copy in halo_copies:
                copy.wait()

            @pl.when(me == 0)
            def _():
                win_ref[0:HALO] = jnp.zeros((HALO, 8, pts), jnp.float32)

            @pl.when(me == count - 1)
            def _():
                win_ref[leaves + HALO :] = jnp.zeros((HALO, 8, pts), jnp.float32)

            run_leaves(win_ref, 0, HALO)
            run_leaves(win_ref, leaves - HALO, leaves)
        for copy in copies:
            copy.wait()
        node_row = chain[bits]
        for mask in range(1, size_of[name]):
            node_row = node_row + recv_ref[recv_at + mask - 1, 4:5, 0:rank]
        for step in range(bits):
            base = recv_at + 2**step - 1
            sibling = recv_ref[base, 0:1, 0:rank]
            for other in range(1, 2**step):
                sibling = sibling + recv_ref[base + other, 0:1, 0:rank]
            targets = [node_col_ref[3 * (level + step) + dim] for dim in range(3)]
            sources = [recv_ref[base, 1 + dim : 2 + dim, 0:rank] for dim in range(3)]
            coupling_ref[level + step] = softened(*targets, *sources) * sibling
        level += bits
        pay_at += bits
        recv_at += size_of[name] - 1

    expansion = total_lanes(coupling_ref[levels - 1])
    for level in range(levels - 2, -1, -1):
        expansion = total_lanes(
            coupling_ref[level] + node_transfer_ref[0, level] * total_rows(eye * expansion)
        )
    expansion_row = total_rows(eye * expansion)

    def finish_step(step, carry):
        for part in range(4):
            leaf = step * 4 + part
            combined = total_lanes(transfer_ref[leaf] * expansion_row) + total_lanes(
                far_acc_ref[leaf]
            )
            row = jnp.concatenate(
                [total_rows(eye * combined), total_rows(interp_ref[leaf] * combined)], axis=1
            )
            out_ref[pl.ds(leaf, 1), :] = out_ref[pl.ds(leaf, 1), :] + row
        return carry

    lax.fori_loop(0, leaves // 4, finish_step, 0)


def on_device(
    sizes,
    points,
    charges,
    interpolant,
    leaf_transfer,
    node_transfer,
    node_points,
    near_list,
    near_count,
    far_list,
):
    leaves, _, pts = points.shape
    rank = interpolant.shape[1]
    levels = node_transfer.shape[1]
    peers = sum(size - 1 for size in sizes)
    smem = pl.BlockSpec(memory_space=pltpu.SMEM)
    vmem = pl.BlockSpec(memory_space=pltpu.VMEM)
    hbm = pl.BlockSpec(memory_space=pl.ANY)
    f32 = jnp.float32
    return pl.pallas_call(
        functools.partial(body, sizes),
        out_shape=jax.ShapeDtypeStruct(charges.shape, f32),
        in_specs=[smem, smem, smem, vmem, vmem, hbm, hbm, vmem, vmem],
        out_specs=vmem,
        scratch_shapes=[
            pltpu.VMEM(interpolant.shape, f32),
            pltpu.VMEM(leaf_transfer.shape, f32),
            pltpu.VMEM(charges.shape, f32),
            pltpu.VMEM((leaves + 2 * HALO, 8, pts), f32),
            pltpu.VMEM((leaves + 2 * HALO, 8, pts), f32),
            pltpu.VMEM((3, pts, pts), f32),
            pltpu.VMEM((leaves, rank, pts), f32),
            pltpu.VMEM((levels, rank, rank), f32),
            pltpu.VMEM((3 * levels, rank, rank), f32),
            pltpu.VMEM((levels, 8, pts), f32),
            pltpu.VMEM((peers, 8, pts), f32),
            pltpu.SemaphoreType.DMA((2,)),
            pltpu.SemaphoreType.DMA((2,)),
            pltpu.SemaphoreType.DMA((2,)),
            pltpu.SemaphoreType.DMA((peers,)),
            pltpu.SemaphoreType.DMA((peers,)),
        ],
        compiler_params=pltpu.CompilerParams(
            collective_id=0, has_side_effects=True, vmem_limit_bytes=40 * 2**20
        ),
    )(
        near_list,
        near_count,
        far_list,
        points,
        charges,
        interpolant,
        leaf_transfer,
        node_transfer,
        node_points,
    )


def solution(mesh):
    sizes = tuple(mesh.shape[name] for name in AXES)
    return jax.shard_map(
        functools.partial(on_device, sizes),
        mesh=mesh,
        in_specs=(
            P(AXES, None, None),
            P(AXES, None),
            P(AXES, None, None),
            P(AXES, None, None),
            P(AXES, None, None, None),
            P(AXES, None, None, None),
            P(AXES, None),
            P(AXES),
            P(AXES, None),
        ),
        out_specs=P(AXES, None),
        check_vma=False,
    )
```

time: 87.1 us -> 33.4 us (0.38)
  matrix products: 34.6 us -> 0 us
  Pallas kernels: 0 us -> 26.8 us
  starting transfers between devices: 17.8 us -> 0 us
  other arithmetic: 13.8 us -> 0 us
  local copies, waits for them, and re-layouts: 13.5 us -> 6.2 us
  waiting for transfers between devices: 5.93 us -> 0 us
    dot_general x34 -> x0, matrix products: 34.6 us -> none  [the longest x8 16.3 us: block_terms(): jnp.einsum('bmpq,bmq->bp', kernel_tiles, weights, precision=HIGHEST)]
    pallas_call x0 -> x1, Pallas kernels: none -> 26.8 us  [on_device(): pl.pallas_call(functools.partial(body, sizes), out_shape=jax.ShapeDtypeSt...]
    ppermute x7 -> x0, starting transfers between devices: 17.8 us -> none  [the longest x5 14.6 us: partner(): return lax.ppermute(value, axis, pairs)]
    reduce_sum x21 -> x0, other arithmetic: 10.7 us -> none  [kernel(): return lax.rsqrt(jnp.sum(spread * spread, axis=-3) + SOFTENING)]
    gather x16 -> x0, local copies, waits for them, and re-layouts: 9.36 us -> none  [the longest x8 4.68 us: block_terms(): sources = window[near_block]]
    unnamed x24 -> x17, local copies, waits for them, and re-layouts: 0.23 us -> 6.2 us
    ppermute x7 -> x0, waiting for transfers between devices: 5.93 us -> none  [the longest x5 5.93 us: partner(): return lax.ppermute(value, axis, pairs)]
    slice x47 -> x0, local copies, waits for them, and re-layouts: 2.07 us -> none  [the longest x1 0.85 us: on_device(): centres[level_index]]
  transfers between devices with their start and end apart: 7 -> 0, of which waited for: 4 -> 0; matrix products, arithmetic and copies ran while one was open for 6% -> 0% of each run, Pallas kernels for 0% -> 0%
where the time goes in v1:
time: 33.4 us; the launch traced here: 33 us
  Pallas kernels  26.8 us (80%)
  local copies, waits for them, and re-layouts  6.2 us (19%)
    pallas_call x1, Pallas kernels, on_device(): pl.pallas_call(functools.partial(body, sizes), out_shape=jax.ShapeDtypeSt...  26.8 us
    unnamed x17, local copies, waits for them, and re-layouts  6.2 us

profile of v1, /device:TPU:0, one launch (start us, length us, event | category | flops | bytes accessed | tf_op | source)
XLA Modules:
  0.0 33.0 jit_solution(1018230235118580634)
XLA Ops:
  0.0 0.0 copy-start.5
  0.0 0.0 copy-start.2
  0.0 0.7 %copy.13.node_points_ref = f32[1,5,3,64]{3,2,1,0:T(4,128)S(1)} copy(f32[1,5,3,64]{3,0,2,1:T(1,128)} %param.14) | data formatting | bytes 7680 | tf_op args[5]
  0.7 0.0 copy-done.5
  0.7 0.1 copy.10.near_ref
  0.8 0.8 %copy.11.far_ref = s32[32,8]{1,0:T(8,128)S(1)} copy(s32[32,8]{0,1:T(8,128)} %param.17) | data formatting | bytes 2048 | tf_op args[8]
  1.6 0.0 copy-start.4
  1.6 0.8 %copy.12.points_ref = f32[32,3,128]{2,1,0:T(4,128)S(1)} copy(f32[32,3,128]{2,0,1:T(8,128)} %param.9) | data formatting | bytes 98304 | tf_op args[0]
  2.4 0.0 copy-done.2
  2.4 0.0 copy-done.4
  2.5 0.0 copy-start
  2.5 1.2 %copy-done = f32[32,64,64]{2,1,0:T(8,128)S(1)} copy-done((f32[32,64,64]{2,1,0:T(8,128)S(1)}, f32[32,64,64]{2,1,0:T(8,128)}, u32[]{:S(2)}) %copy-start) | copy-done | bytes 524312
  3.7 0.0 copy-start.1
  3.7 1.2 %copy-done.1 = f32[32,64,64]{2,1,0:T(8,128)S(1)} copy-done((f32[32,64,64]{2,1,0:T(8,128)S(1)}, f32[32,64,64]{2,1,0:T(8,128)}, u32[]{:S(2)}) %copy-start.1) | copy-done | bytes 524312
  4.9 0.0 copy-start.3
  4.9 0.7 %copy-done.3 = f32[32,128]{1,0:T(8,128)S(1)} copy-done((f32[32,128]{1,0:T(8,128)S(1)}, f32[32,128]{1,0:T(8,128)}, u32[]{:S(2)}) %copy-start.3) | copy-done | bytes 16408
  5.6 26.8 %shard_map.91 = f32[32,128]{1,0:T(8,128)S(1)} custom-call(s32[32,8]{1,0:T(8,128)S(1)} %copy.10.near_ref, s32[32]{0:T(128)S(1)} %copy-done.4, s32[32,8]{1,0:T(8,128)S(1)} %copy.11.far_ref, f32[32,3,128]{2,1,0:T(4,128)S(1)} %copy.12.points_ref, f32[32,128]{1,0:T(8,128)S(1)} %copy-done.3, f32[32,64,64]{2,1,0:T(8,128)S(1)} %copy-done, ...), custom_call_target="tpu_custom_call" | custom-call | tf_op jit(solution)/shard_map/pallas_call | solution.py:329
  32.4 0.6 %copy.15 = f32[32,128]{1,0:T(8,128)} copy(f32[32,128]{1,0:T(8,128)S(1)} %shard_map.91) | data formatting | bytes 32768
Async XLA Ops:
  0.0 0.7 %copy-start.5 = (s32[32,8]{0,1:T(8,128)S(1)}, s32[32,8]{0,1:T(8,128)}, u32[]{:S(2)}) copy-start(s32[32,8]{0,1:T(8,128)} %param.15) | copy-start | bytes 3076
  0.0 2.4 %copy-start.2 = (f32[1,5,64,64]{3,2,1,0:T(8,128)S(1)}, f32[1,5,64,64]{3,2,1,0:T(8,128)}, u32[]{:S(2)}) copy-start(f32[1,5,64,64]{3,2,1,0:T(8,128)} %node_transfer_ref.1) | copy-start | bytes 245764
  1.6 0.9 %copy-start.4 = (s32[32]{0:T(128)S(1)}, s32[32]{0:T(128)}, u32[]{:S(2)}) copy-start(s32[32]{0:T(128)} %count_ref.1) | copy-start | bytes 388
  2.5 1.2 %copy-start = (f32[32,64,64]{2,1,0:T(8,128)S(1)}, f32[32,64,64]{2,1,0:T(8,128)}, u32[]{:S(2)}) copy-start(f32[32,64,64]{2,1,0:T(8,128)} %interp_hbm.1) | copy-start | bytes 1572868
  3.7 1.2 %copy-start.1 = (f32[32,64,64]{2,1,0:T(8,128)S(1)}, f32[32,64,64]{2,1,0:T(8,128)}, u32[]{:S(2)}) copy-start(f32[32,64,64]{2,1,0:T(8,128)} %transfer_hbm.1) | copy-start | bytes 1572868
  4.9 0.7 %copy-start.3 = (f32[32,128]{1,0:T(8,128)S(1)}, f32[32,128]{1,0:T(8,128)}, u32[]{:S(2)}) copy-start(f32[32,128]{1,0:T(8,128)} %charges_ref.1) | copy-start | bytes 49156

commit v2 on v1

--- a/solution.py
+++ b/solution.py
@@ -1,5 +1,4 @@
 import functools
-import math
 
 import jax
 import jax.numpy as jnp
@@ -42,18 +41,25 @@
 
 def body(
     sizes,
+    near_hbm,
+    count_hbm,
+    far_hbm,
+    points_hbm,
+    charges_hbm,
+    interp_hbm,
+    transfer_hbm,
+    node_transfer_hbm,
+    node_points_hbm,
+    out_ref,
     near_ref,
     count_ref,
     far_ref,
     points_ref,
     charges_ref,
-    interp_hbm,
-    transfer_hbm,
+    interp_ref,
+    transfer_ref,
     node_transfer_ref,
     node_points_ref,
-    out_ref,
-    interp_ref,
-    transfer_ref,
     turned_ref,
     own_ref,
     win_ref,
@@ -69,10 +75,10 @@
     tree_send,
     tree_recv,
 ):
-    leaves, _, pts = points_ref.shape
+    leaves, pts = charges_ref.shape
     rank = interp_ref.shape[1]
-    near_slots = near_ref.shape[1]
-    far_slots = far_ref.shape[1]
+    near_slots = near_ref.shape[0]
+    far_slots = far_ref.shape[0]
     levels = node_transfer_ref.shape[1]
     gx, gy, gz = (lax.axis_index(name) for name in AXES)
     nx, ny, nz = sizes
@@ -92,10 +98,24 @@
     left = address((me + count - 1) % count)
     right = address((me + 1) % count)
 
-    interp_copy = pltpu.make_async_copy(interp_hbm, interp_ref, load_sem.at[0])
-    transfer_copy = pltpu.make_async_copy(transfer_hbm, transfer_ref, load_sem.at[1])
-    interp_copy.start()
-    transfer_copy.start()
+    loads = [
+        pltpu.make_async_copy(source, target, load_sem.at[at])
+        for at, (source, target) in enumerate(
+            (
+                (points_hbm, points_ref),
+                (charges_hbm, charges_ref),
+                (interp_hbm, interp_ref),
+                (transfer_hbm, transfer_ref),
+                (node_points_hbm, node_points_ref),
+                (node_transfer_hbm, node_transfer_ref),
+                (near_hbm, near_ref),
+                (count_hbm, count_ref),
+                (far_hbm, far_ref),
+            )
+        )
+    ]
+    for load in loads:
+        load.start()
 
     barrier = pltpu.get_barrier_semaphore()
     greeted = 2
@@ -120,21 +140,37 @@
     eye = unit(rank)
     eye_pts = unit(pts)
 
+    own_ref[...] = jnp.zeros_like(own_ref)
+    pay_ref[...] = jnp.zeros_like(pay_ref)
+    loads[0].wait()
+    loads[1].wait()
     turned_ref[...] = jnp.concatenate(
         [charges_ref[:, rank:], charges_ref[:, :rank]], axis=1
     )
-    own_ref[...] = jnp.zeros_like(own_ref)
-    pay_ref[...] = jnp.zeros_like(pay_ref)
-    own_ref[HALO : HALO + leaves, 0:3, :] = points_ref[...]
-
+
+    def target_step(step, carry):
+        for part in range(4):
+            leaf = step * 4 + part
+            rows = [points_ref[dim, pl.ds(leaf, 1), :] for dim in range(3)]
+            for dim in range(3):
+                own_ref[HALO + leaf, dim : dim + 1, :] = rows[dim]
+            own_ref[HALO + leaf, 3:4, :] = charges_ref[pl.ds(leaf, 1), :]
+            tile = jnp.transpose(jnp.concatenate(rows + [jnp.zeros((5, pts), jnp.float32)], axis=0))
+            for dim in range(3):
+                column_ref[leaf, dim] = jnp.broadcast_to(tile[:, dim : dim + 1], (pts, pts))
+        return carry
+
+    lax.fori_loop(0, leaves // 4, target_step, 0)
+
+    loads[4].wait()
     for level in range(levels):
         for dim in range(3):
             node_col_ref[3 * level + dim] = jnp.broadcast_to(
-                total_lanes(eye * node_points_ref[0, level, dim : dim + 1, :]), (rank, rank)
-            )
-
-    interp_copy.wait()
-    transfer_copy.wait()
+                total_lanes(eye * node_points_ref[level, dim]), (rank, rank)
+            )
+
+    for load in loads[2:4] + loads[5:]:
+        load.wait()
 
     def skeleton_step(step, acc):
         for part in range(4):
@@ -142,7 +178,6 @@
             upper = turned_ref[pl.ds(leaf, 1), :]
             row = charges_ref[pl.ds(leaf, 1), :]
             col = total_lanes(interp_ref[leaf] * upper[:, :rank] + eye * row[:, :rank])
-            own_ref[HALO + leaf, 3:4, :] = row
             own_ref[HALO + leaf, 4:5, 0:rank] = total_rows(eye * col)
             acc = acc + transfer_ref[leaf] * col
         return acc
@@ -173,23 +208,17 @@
         copy.start()
     win_ref[HALO : HALO + leaves] = own_ref[HALO : HALO + leaves]
 
-    def set_targets(leaf):
-        tile = jnp.transpose(own_ref[HALO + leaf])
-        for dim in range(3):
-            column_ref[dim] = jnp.broadcast_to(tile[:, dim : dim + 1], (pts, pts))
-
     low_half = lax.broadcasted_iota(jnp.int32, (8, pts), 1) < rank
 
     def leaf_step(source_ref, leaf):
-        set_targets(leaf)
         live = count_ref[leaf]
-        places = [near_ref[leaf, m] for m in range(near_slots)]
+        places = [near_ref[m, leaf] for m in range(near_slots)]
         weights = [
             jnp.where(m < live, source_ref[places[m], 3:4, :], 0.0) for m in range(near_slots)
         ]
         near_cols = []
         for start in range(0, pts, CHUNK):
-            tx, ty, tz = (column_ref[dim, start : start + CHUNK, :] for dim in range(3))
+            tx, ty, tz = (column_ref[leaf, dim, start : start + CHUNK, :] for dim in range(3))
             total = jnp.zeros((CHUNK, pts), jnp.float32)
             for m in range(near_slots):
                 sx, sy, sz = (source_ref[places[m], dim : dim + 1, :] for dim in range(3))
@@ -199,11 +228,11 @@
         out_ref[pl.ds(leaf, 1), :] = total_rows(eye_pts * near_col)
         pairs = []
         for m in range(0, far_slots, 2):
-            first = source_ref[far_ref[leaf, m]]
-            second = source_ref[far_ref[leaf, m + 1]]
+            first = source_ref[far_ref[m, leaf]]
+            second = source_ref[far_ref[m + 1, leaf]]
             pairs.append(jnp.where(low_half, first, pltpu.roll(second, rank, 1)))
         for start in range(0, rank, CHUNK):
-            tx, ty, tz = (column_ref[dim, start : start + CHUNK, :] for dim in range(3))
+            tx, ty, tz = (column_ref[leaf, dim, start : start + CHUNK, :] for dim in range(3))
             total = jnp.zeros((CHUNK, pts), jnp.float32)
             for pair in pairs:
                 total = total + softened(
@@ -212,11 +241,12 @@
             far_acc_ref[leaf, start : start + CHUNK, :] = total
 
     def run_leaves(source_ref, first, last):
-        def step(leaf, carry):
-            leaf_step(source_ref, leaf)
+        def step(pair, carry):
+            leaf_step(source_ref, first + 2 * pair)
+            leaf_step(source_ref, first + 2 * pair + 1)
             return carry
 
-        lax.fori_loop(first, last, step, 0)
+        lax.fori_loop(0, (last - first) // 2, step, 0)
 
     inner = leaves - 2 * HALO
     level = 0
@@ -234,7 +264,10 @@
                 chain.append(total_rows(node_transfer_ref[0, level + step] * col))
         for step in range(bits):
             pay_ref[pay_at + step, 0:1, 0:rank] = chain[step]
-            pay_ref[pay_at + step, 1:4, 0:rank] = node_points_ref[0, level + step]
+            for dim in range(3):
+                pay_ref[pay_at + step, 1 + dim : 2 + dim, 0:rank] = node_points_ref[
+                    level + step, dim
+                ]
             pay_ref[pay_at + step, 4:5, 0:rank] = chain[bits]
         copies = []
         for mask in range(1, size_of[name]):
@@ -250,9 +283,11 @@
             )
             copy.start()
             copies.append(copy)
-        first = HALO + inner * order // len(phases)
-        last = HALO + inner * (order + 1) // len(phases)
-        run_leaves(own_ref, first, last)
+        if not last_phase:
+            spans = max(len(phases) - 1, 1)
+            first = HALO + inner * order // spans // 2 * 2
+            last = HALO + inner * (order + 1) // spans // 2 * 2
+            run_leaves(own_ref, first, last)
         if last_phase:
             for copy in halo_copies:
                 copy.wait()
@@ -318,39 +353,49 @@
     near_count,
     far_list,
 ):
-    leaves, _, pts = points.shape
+    points = points.transpose(1, 0, 2)
+    node_points = node_points.transpose(1, 2, 0, 3)
+    near_list = near_list.T
+    far_list = far_list.T
+    leaves, pts = charges.shape
     rank = interpolant.shape[1]
     levels = node_transfer.shape[1]
     peers = sum(size - 1 for size in sizes)
-    smem = pl.BlockSpec(memory_space=pltpu.SMEM)
     vmem = pl.BlockSpec(memory_space=pltpu.VMEM)
     hbm = pl.BlockSpec(memory_space=pl.ANY)
     f32 = jnp.float32
     return pl.pallas_call(
         functools.partial(body, sizes),
         out_shape=jax.ShapeDtypeStruct(charges.shape, f32),
-        in_specs=[smem, smem, smem, vmem, vmem, hbm, hbm, vmem, vmem],
+        in_specs=[hbm] * 9,
         out_specs=vmem,
         scratch_shapes=[
+            pltpu.SMEM(near_list.shape, jnp.int32),
+            pltpu.SMEM(near_count.shape, jnp.int32),
+            pltpu.SMEM(far_list.shape, jnp.int32),
+            pltpu.VMEM(points.shape, f32),
+            pltpu.VMEM(charges.shape, f32),
             pltpu.VMEM(interpolant.shape, f32),
             pltpu.VMEM(leaf_transfer.shape, f32),
+            pltpu.VMEM(node_transfer.shape, f32),
+            pltpu.VMEM(node_points.shape, f32),
             pltpu.VMEM(charges.shape, f32),
             pltpu.VMEM((leaves + 2 * HALO, 8, pts), f32),
             pltpu.VMEM((leaves + 2 * HALO, 8, pts), f32),
-            pltpu.VMEM((3, pts, pts), f32),
+            pltpu.VMEM((leaves, 3, pts, pts), f32),
             pltpu.VMEM((leaves, rank, pts), f32),
             pltpu.VMEM((levels, rank, rank), f32),
             pltpu.VMEM((3 * levels, rank, rank), f32),
             pltpu.VMEM((levels, 8, pts), f32),
             pltpu.VMEM((peers, 8, pts), f32),
-            pltpu.SemaphoreType.DMA((2,)),
+            pltpu.SemaphoreType.DMA((9,)),
             pltpu.SemaphoreType.DMA((2,)),
             pltpu.SemaphoreType.DMA((2,)),
             pltpu.SemaphoreType.DMA((peers,)),
             pltpu.SemaphoreType.DMA((peers,)),
         ],
         compiler_params=pltpu.CompilerParams(
-            collective_id=0, has_side_effects=True, vmem_limit_bytes=40 * 2**20
+            collective_id=0, has_side_effects=True, vmem_limit_bytes=63 * 2**20
         ),
     )(
         near_list,

time: 33.4 us -> 24.1 us (0.72)
  local copies, waits for them, and re-layouts: 6.2 us -> 1.32 us
  Pallas kernels: 26.8 us -> 22.5 us
    unnamed x17 -> x1, local copies, waits for them, and re-layouts: 6.2 us -> 1.32 us
    pallas_call x1, Pallas kernels: 26.8 us -> 22.5 us  [on_device(): pl.pallas_call(functools.partial(body, sizes), out_shape=jax.ShapeDtypeSt...]
where the time goes in v2:
time: 24.1 us; the launch traced here: 23.9 us
  Pallas kernels  22.5 us (93%)
  local copies, waits for them, and re-layouts  1.32 us (5%)
    pallas_call x1, Pallas kernels, on_device(): pl.pallas_call(functools.partial(body, sizes), out_shape=jax.ShapeDtypeSt...  22.5 us
    unnamed x1, local copies, waits for them, and re-layouts  1.32 us

profile of v2, /device:TPU:0, one launch (start us, length us, event | category | flops | bytes accessed | tf_op | source)
XLA Modules:
  0.0 23.9 jit_solution(12610614514560050742)
XLA Ops:
  0.0 22.5 %shard_map.91 = f32[32,128]{1,0:T(8,128)} custom-call(s32[8,32]{1,0:T(8,128)} %bitcast.6, s32[32]{0:T(128)} %count_hbm.1, s32[8,32]{1,0:T(8,128)} %bitcast.7, f32[3,32,128]{2,1,0:T(8,128)} %bitcast.4, f32[32,128]{1,0:T(8,128)} %charges_hbm.1, f32[32,64,64]{2,1,0:T(8,128)} %interp_hbm.1, f32[32,64,64]{2,1,0:T(8,128)} %transfer_hbm.1, ...), custom_call_target="tpu_custom_call" | custom-call | tf_op jit(solution)/shard_map/pallas_call | solution.py:367
  22.6 1.3 %copy.11 = f32[32,128]{1,0:T(8,128)} copy(f32[32,128]{1,0:T(8,128)} %shard_map.91) | data formatting | bytes 32768

commit v3 on v2

--- a/solution.py
+++ b/solution.py
@@ -1,4 +1,5 @@
 import functools
+import math
 
 import jax
 import jax.numpy as jnp
@@ -12,6 +13,7 @@
 MESH = pl.DeviceIdType.MESH
 AXES = ("gx", "gy", "gz")
 CHUNK = 32
+GROUP = 8
 
 
 def flipped(place, mask):
@@ -51,6 +53,7 @@
     node_transfer_hbm,
     node_points_hbm,
     out_ref,
+    far_out_ref,
     near_ref,
     count_ref,
     far_ref,
@@ -86,7 +89,24 @@
     me = (gx * ny + gy) * nz + gz
     where_of = {"gx": gx, "gy": gy, "gz": gz}
     size_of = dict(zip(AXES, sizes))
-    phases = [name for name in ("gz", "gy", "gx") if size_of[name] > 1]
+    phases = []
+    for name in ("gz", "gy", "gx"):
+        if size_of[name] == 1:
+            continue
+        if phases and math.prod(size_of[x] for x in phases[-1]) * size_of[name] <= GROUP:
+            phases[-1].append(name)
+        else:
+            phases.append([name])
+    extents = [math.prod(size_of[x] for x in names) for names in phases]
+
+    def peer(names, mask):
+        found = {}
+        for axis in names:
+            part = mask % size_of[axis]
+            mask //= size_of[axis]
+            if part:
+                found[axis] = flipped(where_of[axis], part)
+        return found
 
     def address(index):
         return {
@@ -121,12 +141,12 @@
     greeted = 2
     pl.semaphore_signal(barrier, inc=1, device_id=left, device_id_type=MESH)
     pl.semaphore_signal(barrier, inc=1, device_id=right, device_id_type=MESH)
-    for name in phases:
-        for mask in range(1, size_of[name]):
+    for names, extent in zip(phases, extents):
+        for mask in range(1, extent):
             pl.semaphore_signal(
                 barrier,
                 inc=1,
-                device_id={name: flipped(where_of[name], mask)},
+                device_id=peer(names, mask),
                 device_id_type=MESH,
             )
             greeted += 1
@@ -148,44 +168,24 @@
         [charges_ref[:, rank:], charges_ref[:, :rank]], axis=1
     )
 
-    def target_step(step, carry):
-        for part in range(4):
-            leaf = step * 4 + part
-            rows = [points_ref[dim, pl.ds(leaf, 1), :] for dim in range(3)]
-            for dim in range(3):
-                own_ref[HALO + leaf, dim : dim + 1, :] = rows[dim]
-            own_ref[HALO + leaf, 3:4, :] = charges_ref[pl.ds(leaf, 1), :]
-            tile = jnp.transpose(jnp.concatenate(rows + [jnp.zeros((5, pts), jnp.float32)], axis=0))
-            for dim in range(3):
-                column_ref[leaf, dim] = jnp.broadcast_to(tile[:, dim : dim + 1], (pts, pts))
-        return carry
-
-    lax.fori_loop(0, leaves // 4, target_step, 0)
-
-    loads[4].wait()
-    for level in range(levels):
-        for dim in range(3):
-            node_col_ref[3 * level + dim] = jnp.broadcast_to(
-                total_lanes(eye * node_points_ref[level, dim]), (rank, rank)
-            )
-
-    for load in loads[2:4] + loads[5:]:
+    for load in loads[2:]:
         load.wait()
 
     def skeleton_step(step, acc):
-        for part in range(4):
-            leaf = step * 4 + part
+        for part in range(8):
+            leaf = step * 8 + part
             upper = turned_ref[pl.ds(leaf, 1), :]
             row = charges_ref[pl.ds(leaf, 1), :]
             col = total_lanes(interp_ref[leaf] * upper[:, :rank] + eye * row[:, :rank])
+            for dim in range(3):
+                own_ref[HALO + leaf, dim : dim + 1, :] = points_ref[dim, pl.ds(leaf, 1), :]
+            own_ref[HALO + leaf, 3:4, :] = row
             own_ref[HALO + leaf, 4:5, 0:rank] = total_rows(eye * col)
             acc = acc + transfer_ref[leaf] * col
         return acc
 
-    acc = lax.fori_loop(0, leaves // 4, skeleton_step, jnp.zeros((rank, rank), jnp.float32))
+    acc = lax.fori_loop(0, leaves // 8, skeleton_step, jnp.zeros((rank, rank), jnp.float32))
     node_row = total_rows(acc)
-
-    pl.semaphore_wait(barrier, greeted)
     halo_copies = [
         pltpu.make_async_remote_copy(
             src_ref=own_ref.at[pl.ds(HALO, HALO)],
@@ -204,9 +204,26 @@
             device_id_type=MESH,
         ),
     ]
-    for copy in halo_copies:
-        copy.start()
-    win_ref[HALO : HALO + leaves] = own_ref[HALO : HALO + leaves]
+    def while_first_travels():
+        for copy in halo_copies:
+            copy.start()
+        win_ref[HALO : HALO + leaves] = own_ref[HALO : HALO + leaves]
+        def target_step(step, carry):
+            for part in range(4):
+                leaf = step * 4 + part
+                rows = [points_ref[dim, pl.ds(leaf, 1), :] for dim in range(3)]
+                tile = jnp.transpose(jnp.concatenate(rows + [jnp.zeros((5, pts), jnp.float32)], axis=0))
+                for dim in range(3):
+                    column_ref[leaf, dim] = jnp.broadcast_to(tile[:, dim : dim + 1], (pts, pts))
+            return carry
+
+        lax.fori_loop(0, leaves // 4, target_step, 0)
+
+        for level in range(levels):
+            for dim in range(3):
+                node_col_ref[3 * level + dim] = jnp.broadcast_to(
+                    total_lanes(eye * node_points_ref[level, dim]), (rank, rank)
+                )
 
     low_half = lax.broadcasted_iota(jnp.int32, (8, pts), 1) < rank
 
@@ -252,8 +269,8 @@
     level = 0
     pay_at = 0
     recv_at = 0
-    for order, name in enumerate(phases):
-        bits = size_of[name].bit_length() - 1
+    for order, (names, extent) in enumerate(zip(phases, extents)):
+        bits = extent.bit_length() - 1
         last_phase = order == len(phases) - 1
         chain = [node_row]
         for step in range(bits):
@@ -269,8 +286,10 @@
                     level + step, dim
                 ]
             pay_ref[pay_at + step, 4:5, 0:rank] = chain[bits]
+        if order == 0:
+            pl.semaphore_wait(barrier, greeted)
         copies = []
-        for mask in range(1, size_of[name]):
+        for mask in range(1, extent):
             step = mask.bit_length() - 1
             slot = recv_at + mask - 1
             copy = pltpu.make_async_remote_copy(
@@ -278,13 +297,15 @@
                 dst_ref=recv_ref.at[slot],
                 send_sem=tree_send.at[slot],
                 recv_sem=tree_recv.at[slot],
-                device_id={name: flipped(where_of[name], mask)},
+                device_id=peer(names, mask),
                 device_id_type=MESH,
             )
             copy.start()
             copies.append(copy)
-        if not last_phase:
-            spans = max(len(phases) - 1, 1)
+        if order == 0:
+            while_first_travels()
+        spans = max(len(phases) - 1, 1)
+        if order < spans:
             first = HALO + inner * order // spans // 2 * 2
             last = HALO + inner * (order + 1) // spans // 2 * 2
             run_leaves(own_ref, first, last)
@@ -305,7 +326,7 @@
         for copy in copies:
             copy.wait()
         node_row = chain[bits]
-        for mask in range(1, size_of[name]):
+        for mask in range(1, extent):
             node_row = node_row + recv_ref[recv_at + mask - 1, 4:5, 0:rank]
         for step in range(bits):
             base = recv_at + 2**step - 1
@@ -317,7 +338,7 @@
             coupling_ref[level + step] = softened(*targets, *sources) * sibling
         level += bits
         pay_at += bits
-        recv_at += size_of[name] - 1
+        recv_at += extent - 1
 
     expansion = total_lanes(coupling_ref[levels - 1])
     for level in range(levels - 2, -1, -1):
@@ -327,18 +348,18 @@
     expansion_row = total_rows(eye * expansion)
 
     def finish_step(step, carry):
-        for part in range(4):
-            leaf = step * 4 + part
+        for part in range(8):
+            leaf = step * 8 + part
             combined = total_lanes(transfer_ref[leaf] * expansion_row) + total_lanes(
                 far_acc_ref[leaf]
             )
             row = jnp.concatenate(
                 [total_rows(eye * combined), total_rows(interp_ref[leaf] * combined)], axis=1
             )
-            out_ref[pl.ds(leaf, 1), :] = out_ref[pl.ds(leaf, 1), :] + row
+            far_out_ref[pl.ds(leaf, 1), :] = row
         return carry
 
-    lax.fori_loop(0, leaves // 4, finish_step, 0)
+    lax.fori_loop(0, leaves // 8, finish_step, 0)
 
 
 def on_device(
@@ -360,15 +381,15 @@
     leaves, pts = charges.shape
     rank = interpolant.shape[1]
     levels = node_transfer.shape[1]
-    peers = sum(size - 1 for size in sizes)
+    peers = math.prod(sizes) - 1
     vmem = pl.BlockSpec(memory_space=pltpu.VMEM)
     hbm = pl.BlockSpec(memory_space=pl.ANY)
     f32 = jnp.float32
-    return pl.pallas_call(
+    near_part, far_part = pl.pallas_call(
         functools.partial(body, sizes),
-        out_shape=jax.ShapeDtypeStruct(charges.shape, f32),
+        out_shape=[jax.ShapeDtypeStruct(charges.shape, f32)] * 2,
         in_specs=[hbm] * 9,
-        out_specs=vmem,
+        out_specs=[vmem] * 2,
         scratch_shapes=[
             pltpu.SMEM(near_list.shape, jnp.int32),
             pltpu.SMEM(near_count.shape, jnp.int32),
@@ -408,6 +429,7 @@
         node_transfer,
         node_points,
     )
+    return near_part + far_part
 
 
 def solution(mesh):

time: 24.1 us -> 26.2 us (1.087)
  Pallas kernels: 22.5 us -> 24.6 us
  other arithmetic: 0 us -> 1.34 us
  local copies, waits for them, and re-layouts: 1.32 us -> 0 us
    pallas_call x1, Pallas kernels: 22.5 us -> 24.6 us  [on_device(): pl.pallas_call(functools.partial(body, sizes), out_shape=[jax.ShapeDtypeS...]
    add x0 -> x1, other arithmetic: none -> 1.34 us  [on_device(): return near_part + far_part]
    unnamed x1 -> x0, local copies, waits for them, and re-layouts: 1.32 us -> none
where the time goes in v3:
time: 26.2 us; the launch traced here: 25.9 us
  Pallas kernels  24.6 us (94%)
  other arithmetic  1.34 us (5%)
    pallas_call x1, Pallas kernels, on_device(): pl.pallas_call(functools.partial(body, sizes), out_shape=[jax.ShapeDtypeS...  24.6 us
    add x1, other arithmetic, on_device(): return near_part + far_part  1.34 us

profile of v3, /device:TPU:0, one launch (start us, length us, event | category | flops | bytes accessed | tf_op | source)
XLA Modules:
  0.0 25.9 jit_solution(2333441560910623614)
XLA Ops:
  0.0 24.6 %shard_map.91 = (f32[32,128]{1,0:T(8,128)}, f32[32,128]{1,0:T(8,128)}) custom-call(s32[8,32]{1,0:T(8,128)} %bitcast.6, s32[32]{0:T(128)} %count_hbm.1, s32[8,32]{1,0:T(8,128)} %bitcast.7, f32[3,32,128]{2,1,0:T(8,128)} %bitcast.4, f32[32,128]{1,0:T(8,128)} %charges_hbm.1, f32[32,64,64]{2,1,0:T(8,128)} %interp_hbm.1, f32[32,64,64]{2,1,0:T(8,128)} %transfer_hbm.1, ...), custom_call_target="tpu_custom_call" | custom-call | tf_op jit(solution)/shard_map/pallas_call | solution.py:388
  24.6 1.3 %add.3 = f32[32,128]{1,0:T(8,128)} add(f32[32,128]{1,0:T(8,128)} %get-tuple-element.7, f32[32,128]{1,0:T(8,128)} %get-tuple-element.8) | non-fusion elementwise | flops 4096 | bytes 49152 | tf_op jit(solution)/shard_map/add | solution.py:432

commit v4 on v3

--- a/solution.py
+++ b/solution.py
@@ -168,7 +168,25 @@
         [charges_ref[:, rank:], charges_ref[:, :rank]], axis=1
     )
 
-    for load in loads[2:]:
+    def target_step(step, carry):
+        for part in range(4):
+            leaf = step * 4 + part
+            rows = [points_ref[dim, pl.ds(leaf, 1), :] for dim in range(3)]
+            tile = jnp.transpose(jnp.concatenate(rows + [jnp.zeros((5, pts), jnp.float32)], axis=0))
+            for dim in range(3):
+                column_ref[leaf, dim] = jnp.broadcast_to(tile[:, dim : dim + 1], (pts, pts))
+        return carry
+
+    lax.fori_loop(0, leaves // 4, target_step, 0)
+
+    loads[4].wait()
+    for level in range(levels):
+        for dim in range(3):
+            node_col_ref[3 * level + dim] = jnp.broadcast_to(
+                total_lanes(eye * node_points_ref[level, dim]), (rank, rank)
+            )
+
+    for load in loads[2:4] + loads[5:]:
         load.wait()
 
     def skeleton_step(step, acc):
@@ -208,22 +226,6 @@
         for copy in halo_copies:
             copy.start()
         win_ref[HALO : HALO + leaves] = own_ref[HALO : HALO + leaves]
-        def target_step(step, carry):
-            for part in range(4):
-                leaf = step * 4 + part
-                rows = [points_ref[dim, pl.ds(leaf, 1), :] for dim in range(3)]
-                tile = jnp.transpose(jnp.concatenate(rows + [jnp.zeros((5, pts), jnp.float32)], axis=0))
-                for dim in range(3):
-                    column_ref[leaf, dim] = jnp.broadcast_to(tile[:, dim : dim + 1], (pts, pts))
-            return carry
-
-        lax.fori_loop(0, leaves // 4, target_step, 0)
-
-        for level in range(levels):
-            for dim in range(3):
-                node_col_ref[3 * level + dim] = jnp.broadcast_to(
-                    total_lanes(eye * node_points_ref[level, dim]), (rank, rank)
-                )
 
     low_half = lax.broadcasted_iota(jnp.int32, (8, pts), 1) < rank
 

time: 26.2 us -> 24.4 us (0.931)
  Pallas kernels: 24.6 us -> 22.9 us
    pallas_call x1, Pallas kernels: 24.6 us -> 22.9 us  [on_device(): pl.pallas_call(functools.partial(body, sizes), out_shape=[jax.ShapeDtypeS...]
where the time goes in v4:
time: 24.4 us; the launch traced here: 24.2 us
  Pallas kernels  22.9 us (94%)
  other arithmetic  1.34 us (5%)
    pallas_call x1, Pallas kernels, on_device(): pl.pallas_call(functools.partial(body, sizes), out_shape=[jax.ShapeDtypeS...  22.9 us
    add x1, other arithmetic, on_device(): return near_part + far_part  1.34 us

profile of v4, /device:TPU:0, one launch (start us, length us, event | category | flops | bytes accessed | tf_op | source)
XLA Modules:
  0.0 24.2 jit_solution(16951217663725278855)
XLA Ops:
  0.0 22.9 %shard_map.91 = (f32[32,128]{1,0:T(8,128)}, f32[32,128]{1,0:T(8,128)}) custom-call(s32[8,32]{1,0:T(8,128)} %bitcast.6, s32[32]{0:T(128)} %count_hbm.1, s32[8,32]{1,0:T(8,128)} %bitcast.7, f32[3,32,128]{2,1,0:T(8,128)} %bitcast.4, f32[32,128]{1,0:T(8,128)} %charges_hbm.1, f32[32,64,64]{2,1,0:T(8,128)} %interp_hbm.1, f32[32,64,64]{2,1,0:T(8,128)} %transfer_hbm.1, ...), custom_call_target="tpu_custom_call" | custom-call | tf_op jit(solution)/shard_map/pallas_call | solution.py:390
  22.9 1.3 %add.3 = f32[32,128]{1,0:T(8,128)} add(f32[32,128]{1,0:T(8,128)} %get-tuple-element.7, f32[32,128]{1,0:T(8,128)} %get-tuple-element.8) | non-fusion elementwise | flops 4096 | bytes 49152 | tf_op jit(solution)/shard_map/add | solution.py:434
